TPU v7x, 32 devices: a whole 2x2x4 slice. The times are simulated.
32 devices in a mesh: fsdp: 16 (over z, y, core), tp: 2 (over x).
Axes of the slice: x: 2, y: 2, z: 4, core: 2. Of those that a mesh axis runs over, the one named last changes fastest.
Arguments:
- tokens: bfloat16 [4096, 4096], P('fsdp', 'tp'), may hold values from -6 to 6
- w_feat: bfloat16 [3, 4096, 4096], P(None, 'fsdp', 'tp'), may hold values from -0.09375 to 0.09375
- short_filter: float32 [3, 256, 7], P(None, 'tp'), may hold values from -6 to 6
- long_filter: bfloat16 [256, 128], P('tp'), may hold values from -1.5 to 1.5
- doc_ids: int32 [4096], P('fsdp'), may hold values from 0 to 7, never falling along the last dimension, each value on 1 to 2048 neighbouring positions
- grad_out: bfloat16 [4096, 4096], P('fsdp', 'tp'), may hold values from -6 to 6
Outputs:
- mixed: bfloat16 [4096, 4096], P('fsdp', 'tp')
- input_grad: bfloat16 [4096, 4096], P('fsdp', 'tp')
Inputs may be any that keep to these rules, and one draw needn't show every extreme that they name: `doc_ids`: document numbers never fall along the positions; each document covers 1 to 2048 consecutive positions and one covers exactly 2048; every number from 0 to 7 occurs.
All inputs are finite; a program needn't handle non-finite values.
Results may differ from a plain program's by a relative error of at most 0.0081.
Values may be sent and summed in bfloat16 or wider, within the bound.
A program may use at most 192 MiB of HBM per device.

v0:
```python
import jax
import jax.numpy as jnp
from jax import lax
from jax.sharding import PartitionSpec as P


def shifted_2(value, axis, steps):
    count = lax.axis_size(axis)
    initial, last = (max(0, -steps), min(count, count - steps))
    return lax.ppermute(value, axis, [(source, source + steps) for source in range(initial, last)])


def causal_taps(extended, doc_ext, filters, lead_rows):
    row_count = extended.shape[0] - lead_rows
    doc_now = doc_ext[lead_rows:]
    bcast_shape = (row_count,) + (1,) * (extended.ndim - 1)
    summed = jnp.zeros((row_count,) + extended.shape[1:], jnp.float32)
    for offset in range(filters.shape[-1]):
        shifted = extended[lead_rows - offset : lead_rows - offset + row_count].astype(jnp.float32)
        same_doc = (
            (doc_ext[lead_rows - offset : lead_rows - offset + row_count] == doc_now)
            .astype(jnp.float32)
            .reshape(bcast_shape)
        )
        summed = summed + filters[..., offset] * shifted * same_doc
    return summed


def ahead_taps(extended, doc_ext, filters, row_count):
    doc_now = doc_ext[:row_count]
    bcast_shape = (row_count,) + (1,) * (extended.ndim - 1)
    summed = jnp.zeros((row_count,) + extended.shape[1:], jnp.float32)
    for offset in range(filters.shape[-1]):
        shifted = extended[offset : offset + row_count].astype(jnp.float32)
        same_doc = (
            (doc_ext[offset : offset + row_count] == doc_now)
            .astype(jnp.float32)
            .reshape(bcast_shape)
        )
        summed = summed + filters[..., offset] * shifted * same_doc
    return summed


def toeplitz_base(long_filter, anti_causal):
    tap_count = long_filter.shape[1]
    row_iota = lax.broadcasted_iota(jnp.int32, (tap_count, 2 * tap_count), 0)
    col_iota = lax.broadcasted_iota(jnp.int32, (tap_count, 2 * tap_count), 1)
    if anti_causal:
        lag_index = col_iota - row_iota
    else:
        lag_index = row_iota + tap_count - col_iota
    tap_iota = lax.broadcasted_iota(jnp.int32, (tap_count, tap_count, 2 * tap_count), 0)
    one_hot = (
        (tap_iota == lag_index[None])
        .astype(long_filter.dtype)
        .reshape(tap_count, 2 * tap_count * tap_count)
    )
    table = jnp.dot(long_filter, one_hot, preferred_element_type=jnp.float32).astype(
        long_filter.dtype
    )
    return table.reshape(long_filter.shape[0], tap_count, 2 * tap_count)


def blocked_conv(extended, doc_ext, toeplitz, doc_rows, row_count):
    groups = toeplitz.shape[0]
    tap_count = toeplitz.shape[1]
    chan_width = extended.shape[1]
    block_count = row_count // tap_count
    row_blocks = extended.reshape(block_count + 1, tap_count, chan_width)
    windows = jnp.concatenate([row_blocks[:-1], row_blocks[1:]], axis=1)
    doc_blocks = doc_ext.reshape(block_count + 1, tap_count)
    doc_windows = jnp.concatenate([doc_blocks[:-1], doc_blocks[1:]], axis=1)
    row_docs = doc_rows.reshape(block_count, tap_count)

    def one_block(inputs):
        window, col_docs, own_docs = inputs
        window = window.reshape(2 * tap_count, groups, chan_width // groups)
        kernel = toeplitz * (own_docs[:, None] == col_docs[None, :]).astype(toeplitz.dtype)[None]
        result = jnp.einsum("gtu,ugk->tgk", kernel, window, preferred_element_type=jnp.float32)
        return result.reshape(tap_count, chan_width)

    blocks = lax.map(one_block, (windows, doc_windows, row_docs))
    return blocks.reshape(row_count, chan_width)


def shards(tokens, w_feat, short_filter, long_filter, doc_ids, grad_out):
    rows_here = tokens.shape[0]
    tap_count = long_filter.shape[1]
    margin = 8
    reach_rows = tap_count + margin
    gathered = lax.all_gather(tokens, "tp", axis=1, tiled=True)
    filter_groups = short_filter.shape[1]
    short_full = jnp.broadcast_to(
        short_filter[:, :, None, :], (3, filter_groups, 16, short_filter.shape[2])
    ).reshape(3, filter_groups * 16, short_filter.shape[2])
    w_whole = lax.all_gather(w_feat, "fsdp", axis=1, tiled=True)
    u_all = jnp.einsum("sd,jdc->sjc", gathered, w_whole, preferred_element_type=jnp.float32).astype(
        jnp.bfloat16
    )
    u_pair = u_all[:, 1:]
    prev_pair, prev_doc = shifted_2(
        (u_pair[rows_here - reach_rows :], doc_ids[rows_here - reach_rows :]), "fsdp", 1
    )
    ext_pair = jnp.concatenate([prev_pair, u_pair], axis=0)
    ext_doc = jnp.concatenate([prev_doc, doc_ids], axis=0)
    conv_pair = causal_taps(ext_pair, ext_doc, short_full[1:], margin)
    product_kv = (conv_pair[:, 0] * conv_pair[:, 1]).astype(jnp.bfloat16)
    doc_product = ext_doc[margin:]
    long_out = blocked_conv(
        product_kv, doc_product, toeplitz_base(long_filter, False), doc_ids, rows_here
    )
    conv_pair, long_out, prev_doc = (
        conv_pair[tap_count:],
        long_out,
        prev_doc[reach_rows - margin :],
    )
    u_query = u_all[:, 0]
    prev_query = shifted_2(u_query[rows_here - margin :], "fsdp", 1)
    ext_query = jnp.concatenate([prev_query, u_query], axis=0)
    ext_doc = jnp.concatenate([prev_doc, doc_ids], axis=0)
    conv_query = causal_taps(ext_query, ext_doc, short_full[0], margin)
    pieces = ((0, 3, w_whole),)
    block_out = (conv_query * long_out).astype(jnp.bfloat16)
    grad_float = grad_out.astype(jnp.float32)
    grad_long = (grad_float * conv_query).astype(jnp.bfloat16)
    grad_query = grad_float * long_out
    next_grad, next_doc = shifted_2((grad_long[:tap_count], doc_ids[:tap_count]), "fsdp", -1)
    ext_grad = jnp.concatenate([grad_long, next_grad], axis=0)
    ext_doc = jnp.concatenate([doc_ids, next_doc], axis=0)
    grad_mixed = blocked_conv(
        ext_grad, ext_doc, toeplitz_base(long_filter, True), doc_ids, rows_here
    )
    grad_feat = jnp.stack(
        [grad_query, grad_mixed * conv_pair[:, 1], grad_mixed * conv_pair[:, 0]], axis=1
    ).astype(jnp.bfloat16)
    next_feat = shifted_2(grad_feat[:margin], "fsdp", -1)
    ext_feat = jnp.concatenate([grad_feat, next_feat], axis=0)
    doc_feat = jnp.concatenate([doc_ids, next_doc[:margin]], axis=0)
    grad_u = ahead_taps(ext_feat, doc_feat, short_full, rows_here).astype(jnp.bfloat16)
    first_role, end_role, weights = pieces[0]
    partial_value = jnp.einsum("sjc,jdc->sd", grad_u, weights, preferred_element_type=jnp.float32)
    input_grad = lax.psum_scatter(
        partial_value.astype(jnp.bfloat16), "tp", scatter_dimension=1, tiled=True
    )
    return (block_out, input_grad)


def solution(mesh):
    in_specs = (
        P("fsdp", "tp"),
        P(None, "fsdp", "tp"),
        P(None, "tp", None),
        P("tp", None),
        P("fsdp"),
        P("fsdp", "tp"),
    )
    out_specs = (P("fsdp", "tp"), P("fsdp", "tp"))
    return jax.shard_map(shards, mesh=mesh, in_specs=in_specs, out_specs=out_specs, check_vma=False)
```

profile of v0, /device:TPU:0, one launch (start us, length us, event | category | flops | bytes accessed | tf_op | source)
XLA Modules:
  0.0 490.7 jit_solution(5397390255139693855)
XLA Ops:
  8.8 2.3 collective-permute-start.1
  15.6 4.7 convolution_convert_fusion
  20.4 4.6 convolution_convert_fusion.1
  25.0 12.7 %copy.35 = bf16[128,128,256]{2,1,0:T(8,128)(2,1)} copy(bf16[128,128,256]{0,2,1:T(8,128)(2,1)} %bitcast.135) | data formatting | bytes 16777216 | tf_op jit(solution)/shard_map/while | solution.py:82
  37.7 12.7 %copy.31 = bf16[128,128,256]{2,1,0:T(8,128)(2,1)} copy(bf16[128,128,256]{0,2,1:T(8,128)(2,1)} %bitcast.136) | data formatting | bytes 16777216 | tf_op jit(solution)/shard_map/while | solution.py:82
  50.7 243.4 %all-gather.5.cloned.1.call-done = bf16[3,4096,2048]{2,1,0:T(8,128)(2,1)} async-done(((bf16[3,256,2048]{2,1,0:T(8,128)(2,1)}), bf16[3,4096,2048]{2,1,0:T(8,128)(2,1)}) %all-gather.5.cloned.1.call-update) | async-done | bytes 50331664 | tf_op jit(solution)/shard_map/all_gather | solution.py:96
  294.1 21.2 %convolution_convert_fusion.2 = bf16[256,3,2048]{2,0,1:T(8,128)(2,1)S(1)} fusion(bf16[3,4096,2048]{2,1,0:T(8,128)(2,1)} %all-gather.5.cloned.1.call-done, bf16[256,4096]{1,0:T(8,128)(2,1)} %all-gather.3.cloned.1.call-done), kind=kOutput, calls=%fused_computation.42 | convolution fusion | flops 12886474752 | bytes 55574528 | tf_op jit(solution)/shard_map/sd,jdc->sjc/dot_general | solution.py:97
  315.4 2.2 collective-permute-start
  318.4 4.0 fusion.42
  326.6 4.5 collective-permute-start.2
  336.7 17.0 %while.21 = (s32[]{:T(128)}, f32[2,128,2048]{2,1,0:T(8,128)}, bf16[2,256,2048]{1,2,0:T(8,128)(2,1)}, s32[2,128]{1,0:T(2,128)S(1)}, s32[2,256]{1,0:T(2,128)S(1)}, /*index=5*/bf16[128,128,256]{2,1,0:T(8,128)(2,1)}, s32[]{:T(128)}) while((s32[]{:T(128)}, f32[2,128,2048]{2,1,0:T(8,128)}, bf16[2,256,2048]{1,2,0:T(8,128)(2,1)}, ...), condition=%wide.region_3.4_spmd, body=%wide.region_2.3_spmd.sunk | while | flops 138477568 | bytes 16913496 | solution.py:82
  338.1 5.7 %fusion.83 = f32[128,16,128]{2,1,0:T(8,128)S(1)} fusion(bf16[256,128,16]{0,2,1:T(8,128)(2,1)S(1)} %bitcast.131, bf16[128,128,256]{2,1,0:T(8,128)(2,1)} %get-tuple-element.307, bf16[128,256]{1,0:T(8,128)(2,1)S(1)} %compare_convert_fusion.17), kind=kOutput, calls=%fused_computation.9.clone.1 | convolution fusion | flops 138412032 | bytes 10551296 | tf_op jit(solution)/shard_map/while/body/eval_jaxpr/gtu,ugk->tgk/dot_general | solution.py:79
  346.6 5.7 %fusion.83 = f32[128,16,128]{2,1,0:T(8,128)S(1)} fusion(bf16[256,128,16]{0,2,1:T(8,128)(2,1)S(1)} %bitcast.131, bf16[128,128,256]{2,1,0:T(8,128)(2,1)} %get-tuple-element.307, bf16[128,256]{1,0:T(8,128)(2,1)S(1)} %compare_convert_fusion.17), kind=kOutput, calls=%fused_computation.9.clone.1 | convolution fusion | flops 138412032 | bytes 10551296 | tf_op jit(solution)/shard_map/while/body/eval_jaxpr/gtu,ugk->tgk/dot_general | solution.py:79
  353.8 20.9 %multiply_add_fusion = f32[384,2,2048]{2,0,1:T(8,128)S(1)} fusion(bf16[256,2,2048]{2,0,1:T(8,128)(2,1)} %slice.413, bf16[136,2,2048]{2,0,1:T(8,128)(2,1)} %collective-permute-done.2, f32[384]{0:T(512)S(1)} %get-tuple-element.172, f32[2,2048]{1,0:T(2,128)S(1)} %get-tuple-element.146, f32[384]{0:T(512)S(1)} %get-tuple-element.173, ...), kind=kLoop, calls=%fused_computation.33 | loop fusion | flops 73924608 | bytes 9626624 | tf_op jit(solution)/shard_map/add | solution.py:25
  376.3 1.7 fusion.44
  382.1 2.8 pad_maximum_fusion.3
  386.5 17.0 %while.20 = (s32[]{:T(128)}, f32[2,128,2048]{2,1,0:T(8,128)}, bf16[2,256,2048]{1,2,0:T(8,128)(2,1)}, s32[2,128]{1,0:T(2,128)S(1)}, s32[2,256]{1,0:T(2,128)S(1)}, /*index=5*/bf16[128,128,256]{2,1,0:T(8,128)(2,1)}, s32[]{:T(128)}) while((s32[]{:T(128)}, f32[2,128,2048]{2,1,0:T(8,128)}, bf16[2,256,2048]{1,2,0:T(8,128)(2,1)}, ...), condition=%wide.region_1.2_spmd, body=%wide.region_0.1_spmd.sunk | while | flops 138477568 | bytes 16913496 | solution.py:82
  388.0 5.7 %fusion.79 = f32[128,16,128]{2,1,0:T(8,128)S(1)} fusion(bf16[256,128,16]{0,2,1:T(8,128)(2,1)S(1)} %bitcast.132, bf16[128,128,256]{2,1,0:T(8,128)(2,1)} %get-tuple-element.286, bf16[128,256]{1,0:T(8,128)(2,1)S(1)} %compare_convert_fusion.16), kind=kOutput, calls=%fused_computation.clone.1 | convolution fusion | flops 138412032 | bytes 10551296 | tf_op jit(solution)/shard_map/while/body/eval_jaxpr/gtu,ugk->tgk/dot_general | solution.py:79
  396.4 5.7 %fusion.79 = f32[128,16,128]{2,1,0:T(8,128)S(1)} fusion(bf16[256,128,16]{0,2,1:T(8,128)(2,1)S(1)} %bitcast.132, bf16[128,128,256]{2,1,0:T(8,128)(2,1)} %get-tuple-element.286, bf16[128,256]{1,0:T(8,128)(2,1)S(1)} %compare_convert_fusion.16), kind=kOutput, calls=%fused_computation.clone.1 | convolution fusion | flops 138412032 | bytes 10551296 | tf_op jit(solution)/shard_map/while/body/eval_jaxpr/gtu,ugk->tgk/dot_general | solution.py:79
  403.5 4.2 fusion.41
  409.4 4.1 collective-permute-done.5
  413.5 1.9 pad_maximum_fusion
  415.4 31.4 %fusion.14 = bf16[256,4096]{1,0:T(8,128)(2,1)} fusion(bf16[3,4096,2048]{2,1,0:T(8,128)(2,1)} %all-gather.5.cloned.1.call-done, bf16[264,3,2048]{2,0,1:T(8,128)(2,1)} %pad_maximum_fusion, f32[256]{0:T(256)S(1)} %get-tuple-element.163, f32[3,2048]{1,0:T(4,128)S(1)} %get-tuple-element.187, f32[256]{0:T(256)S(1)} %get-tuple-element.164, ...), kind=kOutput, calls=%fused_computation.35 | convolution fusion | flops 12931563520 | bytes 74627072 | tf_op jit(solution)/shard_map/sjc,jdc->sd/dot_general | solution.py:141
  446.8 37.3 %reduce-scatter.2.cloned.1.call-done = bf16[256,2048]{1,0:T(8,128)(2,1)} async-done(((bf16[256,4096]{1,0:T(8,128)(2,1)}), bf16[256,2048]{1,0:T(8,128)(2,1)}) %reduce-scatter.2.cloned.1.call-update) | async-done | bytes 1048592 | tf_op jit(solution)/shard_map/reduce_scatter | solution.py:142
  (105 shorter events, 37.2 us)
Async XLA Ops:
  7.2 8.5 %copy-start = (bf16[128,128]{1,0:T(8,128)(2,1)S(1)}, bf16[128,128]{1,0:T(8,128)(2,1)}, u32[]{:S(2)}) copy-start(bf16[128,128]{1,0:T(8,128)(2,1)} %param.13) | copy-start | bytes 98308
  7.2 1.6 copy-start.6
  7.2 5.3 %copy-start.5 = (f32[3,128,7]{1,2,0:T(8,128)S(1)}, f32[3,128,7]{1,2,0:T(8,128)}, u32[]{:S(2)}) copy-start(f32[3,128,7]{1,2,0:T(8,128)} %param.12) | copy-start | bytes 32260
  7.2 5.9 %slice-start = ((f32[3,128,7]{1,2,0:T(8,128)}), f32[2,128,7]{1,2,0:T(8,128)S(1)}, s32[]{:S(2)}) async-start(f32[3,128,7]{1,2,0:T(8,128)} %param.12), calls=%async_computation.4 | async-start | bytes 16384 | tf_op jit(solution)/shard_map/slice | solution.py:106
  7.2 43.5 %all-gather.3.cloned.1.call-start = ((), (), s32[]{:S(2)}) async-start(), calls=%async_computation.1 | async-start | bytes 3145728 | tf_op jit(solution)/shard_map/all_gather | solution.py:91
  7.9 286.2 %all-gather.5.cloned.1.call-start = ((), (), s32[]{:S(2)}) async-start(), calls=%async_computation.2 | async-start | bytes 53477376 | tf_op jit(solution)/shard_map/all_gather | solution.py:96
  8.7 475.5 %reduce-scatter.2.cloned.1.call-start = ((), (), s32[]{:S(2)}) async-start(), calls=%async_computation.3 | async-start | bytes 3145728 | tf_op jit(solution)/shard_map/reduce_scatter | solution.py:142
  8.8 41.5 %collective-permute-start.1 = (s32[136]{0:T(256)S(1)}, s32[136]{0:T(256)S(1)}, u32[]{:S(2)}, u32[]{:S(2)}) collective-permute-start(s32[136]{0:T(256)S(1)} %slice.310), channel_id=1, source_target_pairs={{0,2},{2,4},{4,6},{6,8},{8,10},{10,12},{12,14},{14,16},{16,18},{18... | collective-permute-start | bytes 1640 | tf_op jit(solution)/shard_map/ppermute | solution.py:10
  11.2 39.2 %collective-permute-start.4 = (s32[128]{0:T(128)S(1)}, s32[128]{0:T(128)S(1)}, u32[]{:S(2)}, u32[]{:S(2)}) collective-permute-start(s32[128]{0:T(128)S(1)} %slice.367), channel_id=1, source_target_pairs={{2,0},{4,2},{6,4},{8,6},{10,8},{12,10},{14,12},{16,14},{18,16},{20... | collective-permute-start | bytes 1544 | tf_op jit(solution)/shard_map/ppermute | solution.py:10
  50.6 267.7 %copy-start.4 = (bf16[256,2048]{1,0:T(8,128)(2,1)S(1)}, bf16[256,2048]{1,0:T(8,128)(2,1)}, u32[]{:S(2)}) copy-start(bf16[256,2048]{1,0:T(8,128)(2,1)} %param.15) | copy-start | bytes 3145732
  315.4 3.0 collective-permute-start
  322.4 9.4 %collective-permute-start.3 = (bf16[128,2048]{1,0:T(8,128)(2,1)S(1)}, bf16[128,2048]{1,0:T(8,128)(2,1)}, u32[]{:S(2)}, u32[]{:S(2)}) collective-permute-start(bf16[128,2048]{1,0:T(8,128)(2,1)S(1)} %slice.437), channel_id=1, source_target_pairs={{2,0},{4,2},{6,4},{8,6},{10,8},{12,10},{14,12},{16,14},{18,16},{20... | collective-permute-start | bytes 1572872 | tf_op jit(solution)/shard_map/ppermute | solution.py:10
  326.6 27.2 %collective-permute-start.2 = (bf16[136,2,2048]{2,0,1:T(8,128)(2,1)}, bf16[136,2,2048]{2,0,1:T(8,128)(2,1)}, u32[]{:S(2)}, u32[]{:S(2)}) collective-permute-start(bf16[136,2,2048]{2,0,1:T(8,128)(2,1)} %slice.412), channel_id=1, source_target_pairs={{0,2},{2,4},{4,6},{6,8},{8,10},{10,12},{12,14},{14,16},{16,18},{18... | collective-permute-start | bytes 3342344 | tf_op jit(solution)/shard_map/ppermute | solution.py:10
  374.7 1.6 copy-start.3
  403.5 4.2 copy-start.2
  408.0 5.5 %collective-permute-start.5 = (bf16[8,3,2048]{2,0,1:T(8,128)(2,1)S(1)}, bf16[8,3,2048]{2,0,1:T(8,128)(2,1)S(1)}, u32[]{:S(2)}, u32[]{:S(2)}) collective-permute-start(bf16[8,3,2048]{2,0,1:T(8,128)(2,1)S(1)} %slice.441), channel_id=1, source_target_pairs={{2,0},{4,2},{6,4},{8,6},{10,8},{12,10},{14,12},{16,14},{18,16},{20... | collective-permute-start | bytes 294920 | tf_op jit(solution)/shard_map/ppermute | solution.py:10
  415.4 68.7 %copy-start.1 = (bf16[128,128]{1,0:T(8,128)(2,1)S(1)}, bf16[128,128]{1,0:T(8,128)(2,1)}, u32[]{:S(2)}) copy-start(bf16[128,128]{1,0:T(8,128)(2,1)} %param.13) | copy-start | bytes 98308
Sparse Core Ops, SparseCore 0:
  9.6 35.8 all-gather.2
  47.0 247.0 all-gather.4
  446.9 37.1 reduce-scatter.1
where the time goes:
time: 492 us; the launch traced here: 491 us
  waiting for transfers between devices  287 us (58%)
  matrix products  84.6 us (17%)
  local copies, waits for them, and re-layouts  52.1 us (11%)
  other arithmetic  39.6 us (8%)
  between operations  14.1 us (3%)
  starting transfers between devices  13.2 us (3%)
    all_gather x1, waiting for transfers between devices, shards(): w_whole = lax.all_gather(w_feat, 'fsdp', axis=1, tiled=True)  243 us
    reduce_scatter x1, waiting for transfers between devices, shards(): lax.psum_scatter(partial_value.astype(jnp.bfloat16), 'tp', scatter_dimens...  37.3 us
    dot_general x1, matrix products, shards(): jnp.einsum('sjc,jdc->sd', grad_u, weights, preferred_element_type=jnp.flo...  31.4 us
    while x2, local copies, waits for them, and re-layouts, blocked_conv(): blocks = lax.map(one_block, (windows, doc_windows, row_docs))  25.4 us
    dot_general x4, matrix products, one_block(): jnp.einsum('gtu,ugk->tgk', kernel, window, preferred_element_type=jnp.flo...  22.6 us
    dot_general x1, matrix products, shards(): jnp.einsum('sd,jdc->sjc', gathered, w_whole, preferred_element_type=jnp.f...  21.2 us
    add x1, other arithmetic, causal_taps(): summed = summed + filters[..., offset] * shifted * same_doc  20.9 us
    ppermute x6, starting transfers between devices, shifted_2(): lax.ppermute(value, axis, [(source, source + steps) for source in range(i...  13.1 us
  transfers between devices with their start and end apart: 9, of which 4 were waited for; matrix products, arithmetic and copies ran while one was open for 13% of the time, Pallas kernels for 0%

commit v1 on v0

--- a/solution.py
+++ b/solution.py
@@ -93,7 +93,26 @@
     short_full = jnp.broadcast_to(
         short_filter[:, :, None, :], (3, filter_groups, 16, short_filter.shape[2])
     ).reshape(3, filter_groups * 16, short_filter.shape[2])
-    w_whole = lax.all_gather(w_feat, "fsdp", axis=1, tiled=True)
+    current_block, top, near = (lax.axis_size("fsdp"), lax.axis_index("fsdp"), w_feat.shape[1])
+    nodes = tuple((u * current_block if m == 1 else u for m, u in enumerate(w_feat.shape)))
+    w_whole = lax.dynamic_update_slice_in_dim(
+        jnp.zeros(nodes, w_feat.dtype), w_feat, top * near, axis=1
+    )
+    carry = r_now = w_feat
+    for j in [*range(1, current_block // 2 + 1)]:
+        carry = lax.ppermute(
+            carry, "fsdp", tuple(((m, (m + 1) % current_block) for m in range(current_block)))
+        )
+        w_whole = lax.dynamic_update_slice_in_dim(
+            w_whole, carry, (top - j) % current_block * near, axis=1
+        )
+        if 2 * j < current_block:
+            r_now = lax.ppermute(
+                r_now, "fsdp", tuple(((m, (m - 1) % current_block) for m in range(current_block)))
+            )
+            w_whole = lax.dynamic_update_slice_in_dim(
+                w_whole, r_now, (top + j) % current_block * near, axis=1
+            )
     u_all = jnp.einsum("sd,jdc->sjc", gathered, w_whole, preferred_element_type=jnp.float32).astype(
         jnp.bfloat16
     )

time: 492 us -> 769 us (1.56)
  starting transfers between devices: 13.2 us -> 394 us
  waiting for transfers between devices: 287 us -> 103 us
  local copies, waits for them, and re-layouts: 52.1 us -> 128 us
    ppermute x0 -> x15, starting transfers between devices: none -> 349 us  [the longest x8 341 us: shards(): lax.ppermute(carry, 'fsdp', tuple(((m, (m + 1) % current_block) for m in...]
    all_gather x1 -> x0, waiting for transfers between devices: 243 us -> none  [shards(): w_whole = lax.all_gather(w_feat, 'fsdp', axis=1, tiled=True)]
    ppermute x0 -> x15, waiting for transfers between devices: none -> 53.2 us  [the longest x8 53.2 us: shards(): lax.ppermute(carry, 'fsdp', tuple(((m, (m + 1) % current_block) for m in...]
    dynamic_update_slice x0 -> x16, local copies, waits for them, and re-layouts: none -> 51 us  [the longest x8 26.4 us: shards(): lax.dynamic_update_slice_in_dim(w_whole, carry, (top - j) % current_block...]
    ppermute x6, starting transfers between devices: 13.1 us -> 45.6 us  [shifted_2(): lax.ppermute(value, axis, [(source, source + steps) for source in range(i...]
    broadcast_in_dim x0 -> x1, local copies, waits for them, and re-layouts: none -> 16.1 us  [shards(): jnp.zeros(nodes, w_feat.dtype)]
    reduce_scatter x1, waiting for transfers between devices: 37.3 us -> 45.5 us  [shards(): lax.psum_scatter(partial_value.astype(jnp.bfloat16), 'tp', scatter_dimens...]
  transfers between devices with their start and end apart: 9 -> 23, of which waited for: 4 -> 7; matrix products, arithmetic and copies ran while one was open for 13% -> 18% of each run, Pallas kernels for 0% -> 0%
where the time goes in v1:
time: 769 us; the launch traced here: 767 us
  starting transfers between devices  394 us (51%)
  local copies, waits for them, and re-layouts  128 us (17%)
  waiting for transfers between devices  103 us (13%)
  matrix products  84.5 us (11%)
  other arithmetic  42.6 us (6%)
  between operations  14.6 us (2%)
    ppermute x8, starting transfers between devices, shards(): lax.ppermute(carry, 'fsdp', tuple(((m, (m + 1) % current_block) for m in...  341 us
    ppermute x8, waiting for transfers between devices, shards(): lax.ppermute(carry, 'fsdp', tuple(((m, (m + 1) % current_block) for m in...  53.2 us
    ppermute x6, starting transfers between devices, shifted_2(): lax.ppermute(value, axis, [(source, source + steps) for source in range(i...  45.6 us
    reduce_scatter x1, waiting for transfers between devices, shards(): lax.psum_scatter(partial_value.astype(jnp.bfloat16), 'tp', scatter_dimens...  45.5 us
    dot_general x1, matrix products, shards(): jnp.einsum('sjc,jdc->sd', grad_u, weights, preferred_element_type=jnp.flo...  31.3 us
    dynamic_update_slice x8, local copies, waits for them, and re-layouts, shards(): lax.dynamic_update_slice_in_dim(w_whole, carry, (top - j) % current_block...  26.4 us
    while x2, local copies, waits for them, and re-layouts, blocked_conv(): blocks = lax.map(one_block, (windows, doc_windows, row_docs))  25.3 us
    dot_general x4, matrix products, one_block(): jnp.einsum('gtu,ugk->tgk', kernel, window, preferred_element_type=jnp.flo...  22.6 us
  transfers between devices with their start and end apart: 23, of which 7 were waited for; matrix products, arithmetic and copies ran while one was open for 18% of the time, Pallas kernels for 0%

profile of v1, /device:TPU:0, one launch (start us, length us, event | category | flops | bytes accessed | tf_op | source)
XLA Modules:
  0.0 767.2 jit_solution(8759346036366072058)
XLA Ops:
  7.7 5.1 collective-permute-start.1
  12.8 35.2 %collective-permute-done = bf16[3,256,2048]{2,1,0:T(8,128)(2,1)S(1)} collective-permute-done((bf16[3,256,2048]{2,1,0:T(8,128)(2,1)}, bf16[3,256,2048]{2,1,0:T(8,128)(2,1)S(1)}, u32[]{:S(2)}, u32[]{:S(2)}) %collective-permute-start) | collective-permute-done | bytes 3145760 | tf_op jit(solution)/shard_map/ppermute | solution.py:103
  48.0 30.6 %collective-permute-start.2 = (bf16[3,256,2048]{2,1,0:T(8,128)(2,1)S(1)}, bf16[3,256,2048]{2,1,0:T(8,128)(2,1)S(1)}, u32[]{:S(2)}, u32[]{:S(2)}) collective-permute-start(bf16[3,256,2048]{2,1,0:T(8,128)(2,1)S(1)} %collective-permute-done), channel_id=1, source_target_pairs={{0,2},{2,4},{4,6},{6,8},{8,10},{10,12},{12,14},{14,16},{16,18},{18... | collective-permute-start | bytes 9437192 | tf_op jit(solution)/shard_map/ppermute | solution.py:103
  78.6 8.9 %collective-permute-done.2 = bf16[3,256,2048]{2,1,0:T(8,128)(2,1)S(1)} collective-permute-done((bf16[3,256,2048]{2,1,0:T(8,128)(2,1)S(1)}, bf16[3,256,2048]{2,1,0:T(8,128)(2,1)S(1)}, u32[]{:S(2)}, u32[]{:S(2)}) %collective-permute-start.2) | collective-permute-done | bytes 3145760 | tf_op jit(solution)/shard_map/ppermute | solution.py:103
  87.5 60.7 %collective-permute-start.4 = (bf16[3,256,2048]{2,1,0:T(8,128)(2,1)S(1)}, bf16[3,256,2048]{2,1,0:T(8,128)(2,1)S(1)}, u32[]{:S(2)}, u32[]{:S(2)}) collective-permute-start(bf16[3,256,2048]{2,1,0:T(8,128)(2,1)S(1)} %collective-permute-done.2), channel_id=1, source_target_pairs={{0,2},{2,4},{4,6},{6,8},{8,10},{10,12},{12,14},{14,16},{16,18},{18... | collective-permute-start | bytes 9437192 | tf_op jit(solution)/shard_map/ppermute | solution.py:103
  153.5 65.1 %collective-permute-start.6 = (bf16[3,256,2048]{2,1,0:T(8,128)(2,1)S(1)}, bf16[3,256,2048]{2,1,0:T(8,128)(2,1)}, u32[]{:S(2)}, u32[]{:S(2)}) collective-permute-start(bf16[3,256,2048]{2,1,0:T(8,128)(2,1)S(1)} %collective-permute-done.4), channel_id=1, source_target_pairs={{0,2},{2,4},{4,6},{6,8},{8,10},{10,12},{12,14},{14,16},{16,18},{18... | collective-permute-start | bytes 9437192 | tf_op jit(solution)/shard_map/ppermute | solution.py:103
  218.7 5.4 collective-permute-done.6
  224.1 64.4 %collective-permute-start.8 = (bf16[3,256,2048]{2,1,0:T(8,128)(2,1)}, bf16[3,256,2048]{2,1,0:T(8,128)(2,1)}, u32[]{:S(2)}, u32[]{:S(2)}) collective-permute-start(bf16[3,256,2048]{2,1,0:T(8,128)(2,1)} %collective-permute-done.6), channel_id=1, source_target_pairs={{0,2},{2,4},{4,6},{6,8},{8,10},{10,12},{12,14},{14,16},{16,18},{18... | collective-permute-start | bytes 9437192 | tf_op jit(solution)/shard_map/ppermute | solution.py:103
  302.0 57.3 %collective-permute-start.10 = (bf16[3,256,2048]{2,1,0:T(8,128)(2,1)}, bf16[3,256,2048]{2,1,0:T(8,128)(2,1)}, u32[]{:S(2)}, u32[]{:S(2)}) collective-permute-start(bf16[3,256,2048]{2,1,0:T(8,128)(2,1)} %collective-permute-done.8), channel_id=1, source_target_pairs={{0,2},{2,4},{4,6},{6,8},{8,10},{10,12},{12,14},{14,16},{16,18},{18... | collective-permute-start | bytes 9437192 | tf_op jit(solution)/shard_map/ppermute | solution.py:103
  370.1 60.0 %collective-permute-start.12 = (bf16[3,256,2048]{2,1,0:T(8,128)(2,1)}, bf16[3,256,2048]{2,1,0:T(8,128)(2,1)}, u32[]{:S(2)}, u32[]{:S(2)}) collective-permute-start(bf16[3,256,2048]{2,1,0:T(8,128)(2,1)} %collective-permute-done.10), channel_id=1, source_target_pairs={{0,2},{2,4},{4,6},{6,8},{8,10},{10,12},{12,14},{14,16},{16,18},{18... | collective-permute-start | bytes 9437192 | tf_op jit(solution)/shard_map/ppermute | solution.py:103
  430.0 16.1 %broadcast_in_dim.32 = bf16[3,4096,2048]{2,1,0:T(8,128)(2,1)} broadcast(bf16[]{:T(256)} %constant.116.clone.1), dimensions={} | broadcast | bytes 50331648 | tf_op jit(solution)/shard_map/broadcast_in_dim | solution.py:99
  448.1 12.5 %copy.35 = bf16[128,128,256]{2,1,0:T(8,128)(2,1)} copy(bf16[128,128,256]{0,2,1:T(8,128)(2,1)} %bitcast.137) | data formatting | bytes 16777216 | tf_op jit(solution)/shard_map/while | solution.py:82
  460.6 12.8 %copy.31 = bf16[128,128,256]{2,1,0:T(8,128)(2,1)} copy(bf16[128,128,256]{0,2,1:T(8,128)(2,1)} %bitcast.138) | data formatting | bytes 16777216 | tf_op jit(solution)/shard_map/while | solution.py:82
  531.7 21.3 %fusion.41 = bf16[256,3,2048]{2,0,1:T(8,128)(2,1)S(1)} fusion(bf16[3,4096,2048]{2,1,0:T(8,128)(2,1)} %constant_dynamic-update-slice_fusion.2, bf16[256,4096]{1,0:T(8,128)(2,1)} %all-gather.2.cloned.1.call-done), kind=kOutput, calls=%fused_computation.73 | convolution fusion | flops 12886474752 | bytes 55574528 | tf_op jit(solution)/shard_map/sd,jdc->sjc/dot_general | solution.py:116
  553.1 32.7 %collective-permute-start.15 = (bf16[8,2048]{1,0:T(8,128)(2,1)S(1)}, bf16[8,2048]{1,0:T(8,128)(2,1)S(1)}, u32[]{:S(2)}, u32[]{:S(2)}) collective-permute-start(bf16[8,2048]{1,0:T(8,128)(2,1)S(1)} %slice_bitcast_fusion.1), channel_id=1, source_target_pairs={{0,2},{2,4},{4,6},{6,8},{8,10},{10,12},{12,14},{14,16},{16,18},{18... | collective-permute-start | bytes 98312 | tf_op jit(solution)/shard_map/ppermute | solution.py:10
  604.4 17.1 %while.21 = (s32[]{:T(128)}, f32[2,128,2048]{2,1,0:T(8,128)}, bf16[2,256,2048]{1,2,0:T(8,128)(2,1)}, s32[2,128]{1,0:T(2,128)S(1)}, s32[2,256]{1,0:T(2,128)S(1)}, /*index=5*/bf16[128,128,256]{2,1,0:T(8,128)(2,1)}, s32[]{:T(128)}) while((s32[]{:T(128)}, f32[2,128,2048]{2,1,0:T(8,128)}, bf16[2,256,2048]{1,2,0:T(8,128)(2,1)}, ...), condition=%wide.region_3.4_spmd, body=%wide.region_2.3_spmd.sunk | while | flops 138477568 | bytes 16913496 | solution.py:82
  605.8 5.7 fusion.84
  614.3 5.7 fusion.84
  621.5 21.3 %multiply_add_fusion = f32[384,2,2048]{2,0,1:T(8,128)S(1)} fusion(bf16[256,2,2048]{2,0,1:T(8,128)(2,1)} %slice.413, bf16[136,2,2048]{2,0,1:T(8,128)(2,1)} %collective-permute-done.17, f32[384]{0:T(512)S(1)} %get-tuple-element.172, f32[2,2048]{1,0:T(2,128)S(1)} %get-tuple-element.146, f32[384]{0:T(512)S(1)} %get-tuple-element.173, ...), kind=kLoop, calls=%fused_computation.33 | loop fusion | flops 73924608 | bytes 9626624 | tf_op jit(solution)/shard_map/add | solution.py:25
  654.6 16.9 %while.20 = (s32[]{:T(128)}, f32[2,128,2048]{2,1,0:T(8,128)}, bf16[2,256,2048]{1,2,0:T(8,128)(2,1)}, s32[2,128]{1,0:T(2,128)S(1)}, s32[2,256]{1,0:T(2,128)S(1)}, /*index=5*/bf16[128,128,256]{2,1,0:T(8,128)(2,1)}, s32[]{:T(128)}) while((s32[]{:T(128)}, f32[2,128,2048]{2,1,0:T(8,128)}, bf16[2,256,2048]{1,2,0:T(8,128)(2,1)}, ...), condition=%wide.region_1.2_spmd, body=%wide.region_0.1_spmd.sunk | while | flops 138477568 | bytes 16913496 | solution.py:82
  656.0 5.7 fusion.80
  664.5 5.7 fusion.80
  683.5 31.3 %fusion.14 = bf16[256,4096]{1,0:T(8,128)(2,1)} fusion(bf16[3,4096,2048]{2,1,0:T(8,128)(2,1)} %constant_dynamic-update-slice_fusion.2, bf16[264,3,2048]{2,0,1:T(8,128)(2,1)} %pad_maximum_fusion, f32[256]{0:T(256)S(1)} %copy-done.27, f32[3,2048]{1,0:T(4,128)S(1)} %get-tuple-element.187, f32[256]{0:T(256)S(1)} %copy-done.28, ...), kind=kOutput, calls=%fused_computation.35 | convolution fusion | flops 12931563520 | bytes 74627072 | tf_op jit(solution)/shard_map/sjc,jdc->sd/dot_general | solution.py:160
  714.8 45.5 %reduce-scatter.2.cloned.1.call-done = bf16[256,2048]{1,0:T(8,128)(2,1)} async-done(((bf16[256,4096]{1,0:T(8,128)(2,1)}), bf16[256,2048]{1,0:T(8,128)(2,1)}) %reduce-scatter.2.cloned.1.call-update) | async-done | bytes 1048592 | tf_op jit(solution)/shard_map/reduce_scatter | solution.py:161
  (192 shorter events, 143.6 us)
Async XLA Ops:
  7.2 353.0 %copy-start = (bf16[128,128]{1,0:T(8,128)(2,1)S(1)}, bf16[128,128]{1,0:T(8,128)(2,1)}, u32[]{:S(2)}) copy-start(bf16[128,128]{1,0:T(8,128)(2,1)} %param.13) | copy-start | bytes 98308
  7.2 524.6 %all-gather.2.cloned.1.call-start = ((), (), s32[]{:S(2)}) async-start(), calls=%async_computation.1 | async-start | bytes 3145728 | tf_op jit(solution)/shard_map/all_gather | solution.py:91
  7.2 40.8 %collective-permute-start = (bf16[3,256,2048]{2,1,0:T(8,128)(2,1)}, bf16[3,256,2048]{2,1,0:T(8,128)(2,1)S(1)}, u32[]{:S(2)}, u32[]{:S(2)}) collective-permute-start(bf16[3,256,2048]{2,1,0:T(8,128)(2,1)} %param.11), channel_id=1, source_target_pairs={{0,2},{2,4},{4,6},{6,8},{8,10},{10,12},{12,14},{14,16},{16,18},{18... | collective-permute-start | bytes 9437192 | tf_op jit(solution)/shard_map/ppermute | solution.py:103
  7.7 70.9 %collective-permute-start.1 = (bf16[3,256,2048]{2,1,0:T(8,128)(2,1)}, bf16[3,256,2048]{2,1,0:T(8,128)(2,1)S(1)}, u32[]{:S(2)}, u32[]{:S(2)}) collective-permute-start(bf16[3,256,2048]{2,1,0:T(8,128)(2,1)} %param.11), channel_id=1, source_target_pairs={{0,30},{2,0},{4,2},{6,4},{8,6},{10,8},{12,10},{14,12},{16,14},{18,... | collective-permute-start | bytes 9437192 | tf_op jit(solution)/shard_map/ppermute | solution.py:110
  48.0 39.5 %collective-permute-start.2 = (bf16[3,256,2048]{2,1,0:T(8,128)(2,1)S(1)}, bf16[3,256,2048]{2,1,0:T(8,128)(2,1)S(1)}, u32[]{:S(2)}, u32[]{:S(2)}) collective-permute-start(bf16[3,256,2048]{2,1,0:T(8,128)(2,1)S(1)} %collective-permute-done), channel_id=1, source_target_pairs={{0,2},{2,4},{4,6},{6,8},{8,10},{10,12},{12,14},{14,16},{16,18},{18... | collective-permute-start | bytes 9437192 | tf_op jit(solution)/shard_map/ppermute | solution.py:103
  78.6 69.6 %collective-permute-start.3 = (bf16[3,256,2048]{2,1,0:T(8,128)(2,1)S(1)}, bf16[3,256,2048]{2,1,0:T(8,128)(2,1)S(1)}, u32[]{:S(2)}, u32[]{:S(2)}) collective-permute-start(bf16[3,256,2048]{2,1,0:T(8,128)(2,1)S(1)} %collective-permute-done.1), channel_id=1, source_target_pairs={{0,30},{2,0},{4,2},{6,4},{8,6},{10,8},{12,10},{14,12},{16,14},{18,... | collective-permute-start | bytes 9437192 | tf_op jit(solution)/shard_map/ppermute | solution.py:110
  87.5 66.0 %collective-permute-start.4 = (bf16[3,256,2048]{2,1,0:T(8,128)(2,1)S(1)}, bf16[3,256,2048]{2,1,0:T(8,128)(2,1)S(1)}, u32[]{:S(2)}, u32[]{:S(2)}) collective-permute-start(bf16[3,256,2048]{2,1,0:T(8,128)(2,1)S(1)} %collective-permute-done.2), channel_id=1, source_target_pairs={{0,2},{2,4},{4,6},{6,8},{8,10},{10,12},{12,14},{14,16},{16,18},{18... | collective-permute-start | bytes 9437192 | tf_op jit(solution)/shard_map/ppermute | solution.py:103
  149.9 68.8 %collective-permute-start.5 = (bf16[3,256,2048]{2,1,0:T(8,128)(2,1)S(1)}, bf16[3,256,2048]{2,1,0:T(8,128)(2,1)}, u32[]{:S(2)}, u32[]{:S(2)}) collective-permute-start(bf16[3,256,2048]{2,1,0:T(8,128)(2,1)S(1)} %collective-permute-done.3), channel_id=1, source_target_pairs={{0,30},{2,0},{4,2},{6,4},{8,6},{10,8},{12,10},{14,12},{16,14},{18,... | collective-permute-start | bytes 9437192 | tf_op jit(solution)/shard_map/ppermute | solution.py:110
  153.5 70.5 %collective-permute-start.6 = (bf16[3,256,2048]{2,1,0:T(8,128)(2,1)S(1)}, bf16[3,256,2048]{2,1,0:T(8,128)(2,1)}, u32[]{:S(2)}, u32[]{:S(2)}) collective-permute-start(bf16[3,256,2048]{2,1,0:T(8,128)(2,1)S(1)} %collective-permute-done.4), channel_id=1, source_target_pairs={{0,2},{2,4},{4,6},{6,8},{8,10},{10,12},{12,14},{14,16},{16,18},{18... | collective-permute-start | bytes 9437192 | tf_op jit(solution)/shard_map/ppermute | solution.py:103
  218.6 81.1 %collective-permute-start.7 = (bf16[3,256,2048]{2,1,0:T(8,128)(2,1)}, bf16[3,256,2048]{2,1,0:T(8,128)(2,1)}, u32[]{:S(2)}, u32[]{:S(2)}) collective-permute-start(bf16[3,256,2048]{2,1,0:T(8,128)(2,1)} %collective-permute-done.5), channel_id=1, source_target_pairs={{0,30},{2,0},{4,2},{6,4},{8,6},{10,8},{12,10},{14,12},{16,14},{18,... | collective-permute-start | bytes 9437192 | tf_op jit(solution)/shard_map/ppermute | solution.py:110
  224.1 77.9 %collective-permute-start.8 = (bf16[3,256,2048]{2,1,0:T(8,128)(2,1)}, bf16[3,256,2048]{2,1,0:T(8,128)(2,1)}, u32[]{:S(2)}, u32[]{:S(2)}) collective-permute-start(bf16[3,256,2048]{2,1,0:T(8,128)(2,1)} %collective-permute-done.6), channel_id=1, source_target_pairs={{0,2},{2,4},{4,6},{6,8},{8,10},{10,12},{12,14},{14,16},{16,18},{18... | collective-permute-start | bytes 9437192 | tf_op jit(solution)/shard_map/ppermute | solution.py:103
  288.5 471.8 %reduce-scatter.2.cloned.1.call-start = ((), (), s32[]{:S(2)}) async-start(), calls=%async_computation.2 | async-start | bytes 3145728 | tf_op jit(solution)/shard_map/reduce_scatter | solution.py:161
  289.9 186.4 %collective-permute-start.16 = (s32[136]{0:T(256)}, s32[136]{0:T(256)}, u32[]{:S(2)}, u32[]{:S(2)}) collective-permute-start(s32[136]{0:T(256)} %slice.310), channel_id=1, source_target_pairs={{0,2},{2,4},{4,6},{6,8},{8,10},{10,12},{12,14},{14,16},{16,18},{18... | collective-permute-start | bytes 1640 | tf_op jit(solution)/shard_map/ppermute | solution.py:10
  296.2 179.3 %collective-permute-start.19 = (s32[128]{0:T(128)}, s32[128]{0:T(128)}, u32[]{:S(2)}, u32[]{:S(2)}) collective-permute-start(s32[128]{0:T(128)} %slice.367), channel_id=1, source_target_pairs={{2,0},{4,2},{6,4},{8,6},{10,8},{12,10},{14,12},{16,14},{18,16},{20... | collective-permute-start | bytes 1544 | tf_op jit(solution)/shard_map/ppermute | solution.py:10
  299.7 69.7 %collective-permute-start.9 = (bf16[3,256,2048]{2,1,0:T(8,128)(2,1)}, bf16[3,256,2048]{2,1,0:T(8,128)(2,1)}, u32[]{:S(2)}, u32[]{:S(2)}) collective-permute-start(bf16[3,256,2048]{2,1,0:T(8,128)(2,1)} %collective-permute-done.7), channel_id=1, source_target_pairs={{0,30},{2,0},{4,2},{6,4},{8,6},{10,8},{12,10},{14,12},{16,14},{18,... | collective-permute-start | bytes 9437192 | tf_op jit(solution)/shard_map/ppermute | solution.py:110
  302.0 68.1 %collective-permute-start.10 = (bf16[3,256,2048]{2,1,0:T(8,128)(2,1)}, bf16[3,256,2048]{2,1,0:T(8,128)(2,1)}, u32[]{:S(2)}, u32[]{:S(2)}) collective-permute-start(bf16[3,256,2048]{2,1,0:T(8,128)(2,1)} %collective-permute-done.8), channel_id=1, source_target_pairs={{0,2},{2,4},{4,6},{6,8},{8,10},{10,12},{12,14},{14,16},{16,18},{18... | collective-permute-start | bytes 9437192 | tf_op jit(solution)/shard_map/ppermute | solution.py:103
  369.4 115.6 %collective-permute-start.11 = (bf16[3,256,2048]{2,1,0:T(8,128)(2,1)}, bf16[3,256,2048]{2,1,0:T(8,128)(2,1)}, u32[]{:S(2)}, u32[]{:S(2)}) collective-permute-start(bf16[3,256,2048]{2,1,0:T(8,128)(2,1)} %collective-permute-done.9), channel_id=1, source_target_pairs={{0,30},{2,0},{4,2},{6,4},{8,6},{10,8},{12,10},{14,12},{16,14},{18,... | collective-permute-start | bytes 9437192 | tf_op jit(solution)/shard_map/ppermute | solution.py:110
  370.1 118.0 %collective-permute-start.12 = (bf16[3,256,2048]{2,1,0:T(8,128)(2,1)}, bf16[3,256,2048]{2,1,0:T(8,128)(2,1)}, u32[]{:S(2)}, u32[]{:S(2)}) collective-permute-start(bf16[3,256,2048]{2,1,0:T(8,128)(2,1)} %collective-permute-done.10), channel_id=1, source_target_pairs={{0,2},{2,4},{4,6},{6,8},{8,10},{10,12},{12,14},{14,16},{16,18},{18... | collective-permute-start | bytes 9437192 | tf_op jit(solution)/shard_map/ppermute | solution.py:103
  485.0 42.3 %collective-permute-start.13 = (bf16[3,256,2048]{2,1,0:T(8,128)(2,1)}, bf16[3,256,2048]{2,1,0:T(8,128)(2,1)S(1)}, u32[]{:S(2)}, u32[]{:S(2)}) collective-permute-start(bf16[3,256,2048]{2,1,0:T(8,128)(2,1)} %collective-permute-done.11), channel_id=1, source_target_pairs={{0,30},{2,0},{4,2},{6,4},{8,6},{10,8},{12,10},{14,12},{16,14},{18,... | collective-permute-start | bytes 9437192 | tf_op jit(solution)/shard_map/ppermute | solution.py:110
  488.1 41.4 %collective-permute-start.14 = (bf16[3,256,2048]{2,1,0:T(8,128)(2,1)}, bf16[3,256,2048]{2,1,0:T(8,128)(2,1)S(1)}, u32[]{:S(2)}, u32[]{:S(2)}) collective-permute-start(bf16[3,256,2048]{2,1,0:T(8,128)(2,1)} %collective-permute-done.12), channel_id=1, source_target_pairs={{0,2},{2,4},{4,6},{6,8},{8,10},{10,12},{12,14},{14,16},{16,18},{18... | collective-permute-start | bytes 9437192 | tf_op jit(solution)/shard_map/ppermute | solution.py:103
  553.1 33.5 %collective-permute-start.15 = (bf16[8,2048]{1,0:T(8,128)(2,1)S(1)}, bf16[8,2048]{1,0:T(8,128)(2,1)S(1)}, u32[]{:S(2)}, u32[]{:S(2)}) collective-permute-start(bf16[8,2048]{1,0:T(8,128)(2,1)S(1)} %slice_bitcast_fusion.1), channel_id=1, source_target_pairs={{0,2},{2,4},{4,6},{6,8},{8,10},{10,12},{12,14},{14,16},{16,18},{18... | collective-permute-start | bytes 98312 | tf_op jit(solution)/shard_map/ppermute | solution.py:10
  590.7 8.7 %collective-permute-start.18 = (bf16[128,2048]{1,0:T(8,128)(2,1)S(1)}, bf16[128,2048]{1,0:T(8,128)(2,1)}, u32[]{:S(2)}, u32[]{:S(2)}) collective-permute-start(bf16[128,2048]{1,0:T(8,128)(2,1)S(1)} %slice.437), channel_id=1, source_target_pairs={{2,0},{4,2},{6,4},{8,6},{10,8},{12,10},{14,12},{16,14},{18,16},{20... | collective-permute-start | bytes 1572872 | tf_op jit(solution)/shard_map/ppermute | solution.py:10
  594.7 26.8 %collective-permute-start.17 = (bf16[136,2,2048]{2,0,1:T(8,128)(2,1)}, bf16[136,2,2048]{2,0,1:T(8,128)(2,1)}, u32[]{:S(2)}, u32[]{:S(2)}) collective-permute-start(bf16[136,2,2048]{2,0,1:T(8,128)(2,1)} %slice.412), channel_id=1, source_target_pairs={{0,2},{2,4},{4,6},{6,8},{8,10},{10,12},{12,14},{14,16},{16,18},{18... | collective-permute-start | bytes 3342344 | tf_op jit(solution)/shard_map/ppermute | solution.py:10
  676.2 5.3 collective-permute-start.20
  (28 other events, 968.5 us)
Sparse Core Ops, SparseCore 0:
  288.6 34.3 all-gather.1
  714.9 45.3 reduce-scatter.1
